TPU v7x, 32 devices: a whole 2x2x4 slice. The times are simulated.
32 devices in a mesh: st: 8 (over z, x), ch: 4 (over y, core).
Axes of the slice: x: 2, y: 2, z: 4, core: 2. Of those that a mesh axis runs over, the one named last changes fastest.
Arguments:
- waveform: bfloat16 [256, 3, 8704], P('st'), may hold values from -500 to 500
- templates: bfloat16 [416, 32, 512], P('st', 'ch'), may hold values from -50 to 50
- block_of: int32 [4, 416, 2], P('ch'), may hold values from 0 to 7, all different within a row; in each aligned block of 52 rows (0 to 51, 52 to 103, ..., all dimensions but the last counted through in order) at most 17 rows name the same one
- trace_of: int32 [4, 8, 8, 4], P('ch'), may hold values from 0 to 95
Outputs:
- detection: float32 [416, 8192], P('st', 'ch')
Inputs may be any that keep to these rules, and one draw needn't show every extreme that they name: `block_of`: a row names two different station blocks; among the 52 templates of one owner (aligned blocks of the template dimension) in one group, no station block is named by more than 17 templates, and some station block is named by exactly 17.
All inputs are finite; a program needn't handle non-finite values.
Results may differ from a plain program's by a relative error of at most 0.00035.
Values may be sent and summed in bfloat16 or wider, within the bound.
A program may use at most 192 MiB of HBM per device.

v0:
```python
import functools
import math

import jax
import jax.numpy as jnp
from jax import lax
from jax.experimental import pallas as pl
from jax.experimental.pallas import tpu as pltpu
from jax.sharding import PartitionSpec as P

EPSILON = 1e-05
SHIFTS = 32
LANES = 128
GROUP = 17


def correlate_kernel(
    dims,
    me_ref,
    start_ref,
    order_ref,
    gain_ref,
    steps_ref,
    lanes_ref,
    filters_ref,
    keep_ref,
    send_ref,
    totals_ref,
    padded,
    hankel,
    skewed,
    scale,
    turned,
):
    templates, half, taps, used, depth, parts = dims
    block = pl.program_id(0)

    @pl.when(block == 0)
    def _():
        totals_ref[...] = jnp.zeros_like(totals_ref)
        hankel[...] = jnp.zeros_like(hankel)
        padded[...] = jnp.zeros_like(padded)

    low = lax.broadcasted_iota(jnp.int32, (SHIFTS, LANES), 1) < LANES // 2
    whole = taps // LANES
    splits = LANES // SHIFTS

    def ahead(x, by):
        by = (LANES - by) % LANES
        return x if by == 0 else pltpu.roll(x, by, 1)

    def strip(x, m):
        at = (m % splits) * SHIFTS
        return x[at : at + SHIFTS]

    def joined(x, m):
        left = ahead(strip(x, m), m // splits)
        right = ahead(strip(x, m + 1), (m + 1) // splits - LANES // 2)
        return jnp.where(low, left, right)

    for c in range(half):
        padded[:used, :] = lanes_ref[0, c].astype(jnp.float32)
        lanes = padded[...].T
        steps = taps // SHIFTS + 1
        for m in range(steps + 2):
            pair = joined(lanes, m).astype(jnp.bfloat16)
            if m < steps:
                hankel[c, m * SHIFTS : (m + 1) * SHIFTS, :LANES] = pair
            if m >= 2:
                hankel[c, (m - 2) * SHIFTS : (m - 1) * SHIFTS, LANES:] = pair
        squares = lanes * lanes
        high = squares.astype(jnp.bfloat16)
        rest = (squares - high.astype(jnp.float32)).astype(jnp.bfloat16)
        sums = jnp.dot(
            steps_ref[...],
            jnp.concatenate([high, rest], axis=1),
            preferred_element_type=jnp.float32,
        )
        sums = sums[:, :LANES] + sums[:, LANES:]
        before, suffix = sums[:LANES], sums[LANES:]
        total = suffix[0:1]
        middle = jnp.zeros_like(total)
        for by in range(1, whole):
            middle = middle + ahead(total, by)
        energy = suffix + middle + ahead(before, whole)
        root = lax.rsqrt(energy / taps + EPSILON)
        scale[c, :, :LANES] = joined(root, 0)
        scale[c, :, LANES:] = joined(root, 2)

    first, last = start_ref[block], start_ref[block + 1]

    def chunk(number, carry):
        base = first + number * GROUP
        for g in range(GROUP):
            pair = order_ref[base + g]
            rows = filters_ref[pair]
            for c in range(half):
                spread = jnp.broadcast_to(rows[c : c + 1], (SHIFTS, depth))
                spread = pltpu.roll(spread, 0, 1, stride=1, stride_axis=0)
                skewed[c, g * SHIFTS : (g + 1) * SHIFTS, :] = spread.astype(jnp.bfloat16)
        totals = [None] * GROUP
        for c in range(half):
            raw = jnp.dot(skewed[c], hankel[c], preferred_element_type=jnp.float32)
            for g in range(GROUP):
                pair = order_ref[base + g]
                term = raw[g * SHIFTS : (g + 1) * SHIFTS] * (scale[c] * gain_ref[pair * half + c])
                totals[g] = term if c == 0 else totals[g] + term
        for g in range(GROUP):
            place = jnp.where(base + g < last, lax.div(order_ref[base + g], 2), templates)
            totals_ref[place] += totals[g]
        return carry

    lax.fori_loop(0, lax.div(last - first + GROUP - 1, GROUP), chunk, 0)

    @pl.when(block == pl.num_programs(0) - 1)
    def _():
        rows = keep_ref.shape[2]

        batch = turned.shape[0]

        def turn(number, carry):
            for j in range(batch):
                k = number * batch + j
                left, right = totals_ref[k, :, :LANES], totals_ref[k, :, LANES:]
                stack = [left, ahead(left, LANES // 2), right, ahead(right, LANES // 2)]
                turned[j] = jnp.concatenate(stack, axis=0).T[: LANES // 2]
            for slot in range(parts):
                piece = lax.bitwise_xor(me_ref[0], slot)
                at = pl.ds(pl.multiple_of(piece * rows, 8), rows)
                target = send_ref if slot & 1 else keep_ref
                for j in range(batch):
                    target[slot >> 1, number * batch + j] = turned[j, at, :]
            return carry

        lax.fori_loop(0, templates // batch, turn, 0)


def correlate(arrived, filters, sources, axis):
    blocks, half, window = arrived.shape
    templates = filters.shape[0]
    taps = filters.shape[2]
    pairs = templates * 2
    lags = window - taps
    parts = lax.axis_size(axis)
    cols = lags // SHIFTS
    assert cols == 2 * LANES and LANES == 4 * SHIFTS
    used = window // LANES
    depth = -(-(taps + SHIFTS) // LANES) * LANES
    lanes = arrived.reshape(blocks, half, used, LANES)
    wide = filters.astype(jnp.float32)
    gain = 1.0 / (taps * jnp.sqrt(jnp.mean(wide * wide, axis=2) + EPSILON))
    padded = jnp.pad(wide.reshape(pairs, half, taps), ((0, 0), (0, 0), (0, depth - taps)))

    named = sources.reshape(pairs)
    ids = jnp.arange(pairs, dtype=jnp.int32)
    ahead = (named[None, :] < named[:, None]) | (
        (named[None, :] == named[:, None]) & (ids[None, :] < ids[:, None])
    )
    place = jnp.sum(ahead.astype(jnp.int32), axis=1)
    spots = jnp.arange(pairs + GROUP, dtype=jnp.int32)
    order = jnp.sum(jnp.where(place[None, :] == spots[:, None], ids[None, :], 0), axis=1)
    edges = jnp.arange(blocks + 1, dtype=jnp.int32)
    start = jnp.sum((named[None, :] < edges[:, None]).astype(jnp.int32), axis=1)

    spots = jnp.arange(LANES)
    earlier = spots[None, :] < spots[:, None]
    steps = jnp.concatenate([earlier, ~earlier], axis=0).astype(jnp.bfloat16)
    me = lax.axis_index(axis).astype(jnp.int32).reshape(1)
    dims = (templates, half, taps, used, depth, parts)
    smem = pl.BlockSpec(memory_space=pltpu.SMEM)
    piece = (parts // 2, templates, lags // LANES // parts, LANES)
    piece_spec = pl.BlockSpec(piece, lambda b: (0, 0, 0, 0))
    return pl.pallas_call(
        functools.partial(correlate_kernel, dims),
        grid=(blocks,),
        out_shape=[jax.ShapeDtypeStruct(piece, jnp.float32)] * 2,
        in_specs=[
            smem,
            smem,
            smem,
            smem,
            pl.BlockSpec((2 * LANES, LANES), lambda b: (0, 0)),
            pl.BlockSpec((1, half, used, LANES), lambda b: (b, 0, 0, 0)),
            pl.BlockSpec((pairs, half, depth), lambda b: (0, 0, 0)),
        ],
        out_specs=[piece_spec, piece_spec],
        scratch_shapes=[
            pltpu.VMEM((templates + 1, SHIFTS, cols), jnp.float32),
            pltpu.VMEM((LANES, LANES), jnp.float32),
            pltpu.VMEM((half, depth, cols), jnp.bfloat16),
            pltpu.VMEM((half, GROUP * SHIFTS, depth), jnp.bfloat16),
            pltpu.VMEM((half, SHIFTS, cols), jnp.float32),
            pltpu.VMEM((math.gcd(templates, 13), LANES // 2, LANES), jnp.float32),
        ],
        compiler_params=pltpu.CompilerParams(vmem_limit_bytes=40 * 1024 * 1024),
        name="correlate",
    )(me, start, order, gain.reshape(-1), steps, lanes, padded)


def swapped(x, axis, bit):
    return lax.ppermute(x, axis, [(i, i ^ bit) for i in range(lax.axis_size(axis))])


def per_device(waveform, templates, block_of, trace_of):
    own_index = lax.axis_index("st")
    station_count = lax.axis_size("st")
    own_templates = templates.shape[0]
    group_chans = templates.shape[1]
    half_chans = group_chans // 2
    window = waveform.shape[2]
    sources = block_of[0].reshape(station_count, own_templates, 2)
    own_sources = lax.dynamic_index_in_dim(sources, own_index, 0, keepdims=False)
    wanted = lax.dynamic_index_in_dim(trace_of[0], own_index, 1, keepdims=False)
    wanted = wanted.reshape(-1)
    station = (wanted * 43691) >> 17
    source_rows = waveform[station, wanted - 3 * station]
    arrived = lax.all_to_all(
        source_rows.reshape(station_count, half_chans, window),
        "st",
        split_axis=0,
        concat_axis=0,
        tiled=True,
    )
    keep, send = correlate(arrived, templates, own_sources, "ch")
    bit = 1
    while True:
        keep = keep + swapped(send, "ch", bit)
        if keep.shape[0] == 1:
            break
        halves = keep.reshape(keep.shape[0] // 2, 2, *keep.shape[1:])
        keep, send = halves[:, 0], halves[:, 1]
        bit *= 2
    return keep.reshape(own_templates, -1)


def solution(mesh):
    in_specs = (
        P("st", None, None),
        P("st", "ch", None),
        P("ch", None, None),
        P("ch", None, None, None),
    )
    out_specs = P("st", "ch")
    return jax.shard_map(
        per_device, mesh=mesh, in_specs=in_specs, out_specs=out_specs, check_vma=False
    )
```

profile of v0, /device:TPU:0, one launch (start us, length us, event | category | flops | bytes accessed | tf_op | source)
XLA Modules:
  0.0 65.3 jit_solution(4682482397738081655)
XLA Ops:
  0.0 1.1 %dynamic-slice_reduce_fusion = s32[8,4]{1,0:T(8,128)S(1)} fusion(s32[1,8,8,4]{2,3,1,0:T(4,128)} %param.7, s32[]{:T(128)S(6)} %select_n.30), kind=kLoop, calls=%fused_computation.16 | loop fusion | bytes 260 | tf_op jit(solution)/shard_map/jit(dynamic_index_in_dim)/dynamic_slice | solution.py:213
  1.1 0.1 reshape.86
  1.2 0.2 copy-done
  1.5 2.2 %gather_fusion = bf16[32,8704]{1,0:T(8,128)(2,1)S(1)} fusion(bf16[32,3,8704]{2,0,1:T(8,128)(2,1)S(1)} %copy-done, s32[32]{0:T(128)S(1)} %fusion.10), kind=kCustom, calls=%fused_computation | custom fusion | bytes 1114368 | tf_op jit(solution)/shard_map/gather | solution.py:216
  3.7 0.9 %reshape.87 = bf16[8,4,8704]{2,1,0:T(4,128)(2,1)} reshape(bf16[32,8704]{1,0:T(8,128)(2,1)S(1)} %gather_fusion) | data formatting | bytes 1114112 | tf_op jit(solution)/shard_map/reshape | solution.py:218
  4.6 7.3 %all-to-all-start = ((bf16[8,4,8704]{2,1,0:T(4,128)(2,1)}), bf16[8,4,8704]{2,1,0:T(4,128)(2,1)}, u32[]{:S(2)}, u32[]{:S(2)}) async-start(bf16[8,4,8704]{2,1,0:T(4,128)(2,1)} %reshape.87), calls=%async_computation | async-start | bytes 1114112 | tf_op jit(solution)/shard_map/all_to_all | solution.py:217
  12.0 0.1 copy.25
  12.1 0.1 lt.87
  12.2 1.2 %reshape.89 = f32[104,4,512]{2,1,0:T(4,128)} reshape(bf16[52,8,512]{2,1,0:T(8,128)(2,1)S(1)} %copy-done.1) | data formatting | bytes 1277952 | tf_op jit(solution)/shard_map/reshape | solution.py:152
  13.4 0.2 multiply_reduce_fusion
  13.7 0.1 copy.21
  13.8 0.1 reshape.93.gain_ref
  13.9 1.3 %pad.4.filters_ref = f32[104,4,640]{2,1,0:T(4,128)S(1)} pad(f32[104,4,512]{2,1,0:T(4,128)} %reshape.89, f32[]{:T(128)} %constant.13.clone.1), padding=0_0x0_0x0_128 | pad | bytes 1916932 | tf_op jit(solution)/shard_map/jit(_pad)/pad | solution.py:152
  15.2 0.1 convert_reduce_fusion.1.start_ref
  15.4 0.2 convert_reduce_fusion
  15.5 0.1 select_reduce_fusion.order_ref
  15.6 11.6 %all-to-all-done = bf16[8,4,8704]{2,1,0:T(4,128)(2,1)} async-done(((bf16[8,4,8704]{2,1,0:T(4,128)(2,1)}), bf16[8,4,8704]{2,1,0:T(4,128)(2,1)}, u32[]{:S(2)}, u32[]{:S(2)}) %all-to-all-start) | async-done | bytes 557088 | tf_op jit(solution)/shard_map/all_to_all | solution.py:217
  27.2 1.5 %reshape.100.lanes_ref = bf16[8,4,68,128]{3,2,1,0:T(8,128)(2,1)S(1)} reshape(bf16[8,4,8704]{2,1,0:T(4,128)(2,1)} %all-to-all-done) | data formatting | bytes 1114112 | tf_op jit(solution)/shard_map/reshape | solution.py:149
  28.7 21.1 %correlate.1 = (f32[2,52,16,128]{3,2,1,0:T(8,128)S(1)}, f32[2,52,16,128]{3,2,1,0:T(8,128)S(1)}) custom-call(s32[1]{0:T(128)} %bitcast.me_ref, s32[9]{0:T(128)S(1)} %convert_reduce_fusion.1.start_ref, s32[121]{0:T(128)S(1)} %select_reduce_fusion.order_ref, f32[416]{0:T(512)S(1)} %reshape.93.gain_ref, bf16[256,128]{1,0:T(8,128)(2,1)S(1)} %add_convert_fusion.steps_ref, ...), custom_call_target="tpu_custom_call" | custom-call | tf_op jit(solution)/shard_map/correlate/pallas_call | solution.py:173
  49.9 2.4 %collective-permute-done = f32[2,52,16,128]{3,2,1,0:T(8,128)S(1)} collective-permute-done((f32[2,52,16,128]{3,2,1,0:T(8,128)S(1)}, f32[2,52,16,128]{3,2,1,0:T(8,128)S(1)}, u32[]{:S(2)}, u32[]{:S(2)}) %collective-permute-start) | collective-permute-done | bytes 852000 | tf_op jit(solution)/shard_map/ppermute | solution.py:201
  52.3 0.1 add_bitcast_fusion
  52.4 1.6 %collective-permute-start.1 = (f32[1,52,16,128]{3,2,1,0:T(8,128)S(1)}, f32[1,52,16,128]{3,2,1,0:T(8,128)S(1)}, u32[]{:S(2)}, u32[]{:S(2)}) collective-permute-start(f32[1,52,16,128]{3,2,1,0:T(8,128)S(1)} %slice_bitcast_fusion), channel_id=1, source_target_pairs={{0,2},{1,3},{2,0},{3,1},{4,6},{5,7},{6,4},{7,5},{8,10},{9,11},{10,... | collective-permute-start | bytes 1277960 | tf_op jit(solution)/shard_map/ppermute | solution.py:201
  54.0 10.3 %collective-permute-done.1 = f32[1,52,16,128]{3,2,1,0:T(8,128)S(1)} collective-permute-done((f32[1,52,16,128]{3,2,1,0:T(8,128)S(1)}, f32[1,52,16,128]{3,2,1,0:T(8,128)S(1)}, u32[]{:S(2)}, u32[]{:S(2)}) %collective-permute-start.1) | collective-permute-done | bytes 426016 | tf_op jit(solution)/shard_map/ppermute | solution.py:201
  64.4 0.9 %copy.26 = f32[7,8,16,128]{3,1,2,0:T(8,128)} copy(f32[7,8,16,128]{3,2,1,0:T(8,128)S(1)} %bitcast.20) | data formatting | bytes 917504
  (16 shorter events, 0.4 us)
Async XLA Ops:
  0.0 1.5 %copy-start = (bf16[32,3,8704]{2,0,1:T(8,128)(2,1)S(1)}, bf16[32,3,8704]{2,0,1:T(8,128)(2,1)}, u32[]{:S(2)}) copy-start(bf16[32,3,8704]{2,0,1:T(8,128)(2,1)} %param.4) | copy-start | bytes 5013508
  3.7 8.2 %copy-start.2 = (s32[1,416,2]{1,2,0:T(2,128)S(1)}, s32[1,416,2]{1,2,0:T(2,128)}, u32[]{:S(2)}) copy-start(s32[1,416,2]{1,2,0:T(2,128)} %param.6) | copy-start | bytes 9988
  3.7 8.5 %copy-start.1 = (bf16[52,8,512]{2,1,0:T(8,128)(2,1)S(1)}, bf16[52,8,512]{2,1,0:T(8,128)(2,1)}, u32[]{:S(2)}) copy-start(bf16[52,8,512]{2,1,0:T(8,128)(2,1)} %param.5) | copy-start | bytes 1277956
  4.6 22.5 %all-to-all-start = ((bf16[8,4,8704]{2,1,0:T(4,128)(2,1)}), bf16[8,4,8704]{2,1,0:T(4,128)(2,1)}, u32[]{:S(2)}, u32[]{:S(2)}) async-start(bf16[8,4,8704]{2,1,0:T(4,128)(2,1)} %reshape.87), calls=%async_computation | async-start | bytes 1114112 | tf_op jit(solution)/shard_map/all_to_all | solution.py:217
  49.8 2.4 %collective-permute-start = (f32[2,52,16,128]{3,2,1,0:T(8,128)S(1)}, f32[2,52,16,128]{3,2,1,0:T(8,128)S(1)}, u32[]{:S(2)}, u32[]{:S(2)}) collective-permute-start(f32[2,52,16,128]{3,2,1,0:T(8,128)S(1)} %get-tuple-element.8), channel_id=1, source_target_pairs={{0,1},{1,0},{2,3},{3,2},{4,5},{5,4},{6,7},{7,6},{8,9},{9,8},{10,11... | collective-permute-start | bytes 2555912 | tf_op jit(solution)/shard_map/ppermute | solution.py:201
  52.4 11.9 %collective-permute-start.1 = (f32[1,52,16,128]{3,2,1,0:T(8,128)S(1)}, f32[1,52,16,128]{3,2,1,0:T(8,128)S(1)}, u32[]{:S(2)}, u32[]{:S(2)}) collective-permute-start(f32[1,52,16,128]{3,2,1,0:T(8,128)S(1)} %slice_bitcast_fusion), channel_id=1, source_target_pairs={{0,2},{1,3},{2,0},{3,1},{4,6},{5,7},{6,4},{7,5},{8,10},{9,11},{10,... | collective-permute-start | bytes 1277960 | tf_op jit(solution)/shard_map/ppermute | solution.py:201
where the time goes:
time: 65.6 us; the launch traced here: 65.3 us
  waiting for transfers between devices  24.3 us (37%)
  Pallas kernels  21.1 us (32%)
  local copies, waits for them, and re-layouts  10.1 us (15%)
  starting transfers between devices  8.9 us (14%)
  other arithmetic  0.78 us (1%)
    pallas_call x1, Pallas kernels, correlate(): pl.pallas_call(functools.partial(correlate_kernel, dims), grid=(blocks,),...  21.1 us
    ppermute x2, waiting for transfers between devices, swapped(): lax.ppermute(x, axis, [(i, i ^ bit) for i in range(lax.axis_size(axis))])  12.7 us
    all_to_all x1, waiting for transfers between devices, per_device(): lax.all_to_all(source_rows.reshape(station_count, half_chans, window), 's...  11.6 us
    all_to_all x1, starting transfers between devices, per_device(): lax.all_to_all(source_rows.reshape(station_count, half_chans, window), 's...  7.25 us
    gather x1, local copies, waits for them, and re-layouts, per_device(): source_rows = waveform[station, wanted - 3 * station]  2.21 us
    ppermute x2, starting transfers between devices, swapped(): lax.ppermute(x, axis, [(i, i ^ bit) for i in range(lax.axis_size(axis))])  1.65 us
    reshape x1, local copies, waits for them, and re-layouts, correlate(): lanes = arrived.reshape(blocks, half, used, LANES)  1.48 us
    pad x1, local copies, waits for them, and re-layouts, correlate(): jnp.pad(wide.reshape(pairs, half, taps), ((0, 0), (0, 0), (0, depth - tap...  1.33 us
  transfers between devices with their start and end apart: 3, of which 3 were waited for; matrix products, arithmetic and copies ran while one was open for 6% of the time, Pallas kernels for 0%

commit v1 on v0

v1 whole, which is shorter than its diff:
```python
import functools

import jax
import jax.numpy as jnp
import numpy as np
from jax import lax
from jax.experimental import pallas as pl
from jax.experimental.pallas import tpu as pltpu
from jax.sharding import PartitionSpec as P

EPSILON = 1e-05
SHIFTS = 16
LANES = 128
TURNS = LANES // SHIFTS
STEP = 4
MESH = pl.DeviceIdType.MESH
F32 = jnp.float32
BF16 = jnp.bfloat16


def flipped(me, i, size):
    out, k = 0, 1
    while k < size:
        out = out + k * lax.rem(lax.div(me, k) + lax.div(i, k), 2)
        k *= 2
    return out


def kernel(
    dims,
    order_ref,
    place_ref,
    select_ref,
    wave_ref,
    filters_ref,
    steps_ref,
    out_ref,
    stage,
    send,
    recv,
    skew,
    gains,
    plain,
    rolled,
    suffix,
    before,
    total,
    right,
    scale,
    parts,
    turned,
    near_recv,
    far_send,
    far_recv,
    summed,
    send_sem,
    recv_sem,
    near_send_sem,
    near_recv_sem,
    far_send_sem,
    far_recv_sem,
):
    blocks, slots, templates, half, taps, used, depth, lags, chunk, lag = dims
    me = lax.axis_index("st")
    mine = lax.axis_index("ch")
    near, far = flipped(mine, 1, 4), flipped(mine, 2, 4)
    rows = half * used

    barrier = pltpu.get_barrier_semaphore()

    def greet(i, carry):
        pl.semaphore_signal(
            barrier, inc=1, device_id={"st": flipped(me, i, blocks)}, device_id_type=MESH
        )
        return carry

    lax.fori_loop(1, blocks, greet, 0)
    for other in (near, far):
        pl.semaphore_signal(barrier, inc=1, device_id={"ch": other}, device_id_type=MESH)

    wide = 4 * LANES

    def gather(i, carry):
        at = pl.ds(pl.multiple_of(i * wide, wide), wide)
        tile = jnp.dot(select_ref[...], wave_ref[:, at], preferred_element_type=F32)
        for j in range(4):
            spots = pl.ds(i * 4 + j, blocks * half, stride=used)
            stage[spots, :] = tile[:, j * LANES : (j + 1) * LANES]
        return carry

    lax.fori_loop(0, used * LANES // wide, gather, 0)

    def staged(block):
        return stage[pl.ds(pl.multiple_of(block * rows, 16), rows), :].astype(BF16)

    pl.semaphore_wait(barrier, blocks + 1)

    def trace_copy(i):
        other = flipped(me, i, blocks)
        return pltpu.make_async_remote_copy(
            src_ref=send.at[other],
            dst_ref=recv.at[me],
            send_sem=send_sem.at[i],
            recv_sem=recv_sem.at[i],
            device_id={"st": other},
            device_id_type=MESH,
        )

    def post(i, carry):
        other = flipped(me, i, blocks)
        send[other] = staged(other)
        trace_copy(i).start()
        return carry

    lax.fori_loop(1, blocks, post, 0)
    recv[me] = staged(me)

    def spread(k, carry):
        taken = filters_ref[k].astype(F32)
        mean = jnp.sum(taken * taken, axis=1, keepdims=True) / taps
        gain = 1.0 / (taps * jnp.sqrt(mean + EPSILON))
        gain = jnp.broadcast_to(gain, (2 * half, LANES))
        longer = jnp.concatenate([taken, jnp.zeros((2 * half, depth - taps), F32)], axis=1)
        for c in range(2 * half):
            wave = jnp.broadcast_to(longer[c : c + 1], (SHIFTS, depth))
            wave = pltpu.roll(wave, 0, 1, stride=1, stride_axis=0)
            skew[2 * k + c // half, c % half] = wave.astype(BF16)
        gains[2 * k] = gain[:half]
        gains[2 * k + 1] = gain[half:]
        return carry

    lax.fori_loop(0, templates, spread, 0)

    lane = lax.broadcasted_iota(jnp.int32, (SHIFTS, LANES), 1)
    low = lane < LANES // 2
    plain[rows:, :] = jnp.zeros((8, LANES), F32)
    rolled[:, rows:, :] = jnp.zeros((TURNS - 1, 8, LANES), F32)
    extra = depth // LANES

    def prepare(source):
        x = recv[source].astype(F32)
        plain[:rows, :] = x
        squares = x * x
        high = squares.astype(BF16)
        rest = (squares - high.astype(F32)).astype(BF16)
        sums = jnp.dot(
            jnp.concatenate([high, rest], axis=1), steps_ref[...], preferred_element_type=F32
        )
        suffix[:rows, :] = sums[:, :LANES]
        before[:rows, :] = sums[:, LANES : 2 * LANES]
        total[:rows, :] = sums[:, 2 * LANES :]
        for m in range(1, TURNS):
            rolled[m - 1, :rows, :] = pltpu.roll(x, LANES - SHIFTS * m, 1)
        for c in range(half):
            for m in range(TURNS):
                held = plain if m == 0 else rolled.at[m - 1]
                found = [
                    held[pl.ds(c * used + b, SHIFTS, stride=STEP), :]
                    for b in range(STEP + extra - (m == 0))
                ]
                for b in range(STEP + extra - 1):
                    tile = found[b]
                    if m > 0:
                        tile = jnp.where(lane < LANES - SHIFTS * m, tile, found[b + 1])
                    right[c, m * TURNS + b] = tile.astype(BF16)
        for c in range(0, half, 2):
            roots = []
            for d in (c, c + 1):
                for b in range(STEP):
                    base = d * used + b
                    energy = suffix[pl.ds(base, SHIFTS, stride=STEP), :]
                    for q in range(1, taps // LANES):
                        energy = energy + total[pl.ds(base + q, SHIFTS, stride=STEP), :]
                    energy = energy + before[pl.ds(base + taps // LANES, SHIFTS, stride=STEP), :]
                    roots.append(lax.rsqrt(energy / taps + EPSILON))
            roots = jnp.concatenate(roots, axis=0).T
            for t in range(TURNS // 2):
                even = roots[2 * t * SHIFTS : (2 * t + 1) * SHIFTS]
                odd = roots[(2 * t + 1) * SHIFTS : (2 * t + 2) * SHIFTS]
                at = slice(t * LANES, (t + 1) * LANES)
                scale[c, :, at] = jnp.where(low, even, pltpu.roll(odd, LANES // 2, 1))
                scale[c + 1, :, at] = jnp.where(low, pltpu.roll(even, LANES // 2, 1), odd)

    def products(source):
        base = source * slots
        for c in range(half):
            left = jnp.concatenate([skew[order_ref[base + g], c] for g in range(slots)], axis=0)
            tiles = []
            for m in range(TURNS):
                for b in range(STEP):
                    tiles.append(
                        jnp.concatenate(
                            [right[c, m * TURNS + b + q] for q in range(extra)], axis=1
                        )
                    )
            raw = lax.dot_general(
                left,
                jnp.concatenate(tiles, axis=0),
                (((1,), (1,)), ((), ())),
                preferred_element_type=F32,
            )
            for g in range(slots):
                gain = gains[order_ref[base + g], pl.ds(c, 1), :]
                gain = jnp.concatenate([gain] * (lags // SHIFTS // LANES), axis=1)
                term = raw[g * SHIFTS : (g + 1) * SHIFTS] * (scale[c] * gain)
                if c == 0:
                    parts[base + g] = term
                else:
                    parts[base + g] += term

    def work(i, carry):
        source = flipped(me, i, blocks)

        @pl.when(i > 0)
        def _():
            trace_copy(i).wait_recv()

        prepare(source)
        products(source)
        return carry

    lax.fori_loop(0, blocks, work, 0)

    piece = lags // LANES // 4
    chunks = templates // chunk

    def some(j):
        return pl.ds(j * chunk, chunk)

    def spots(number):
        return pl.ds(pl.multiple_of(number * piece, 8), piece)

    def near_copy(j, side):
        number = lax.rem(near, 2) + 2 * side
        return pltpu.make_async_remote_copy(
            src_ref=turned.at[some(j), spots(number)],
            dst_ref=near_recv.at[side, some(j)],
            send_sem=near_send_sem.at[j, side],
            recv_sem=near_recv_sem.at[j, side],
            device_id={"ch": near},
            device_id_type=MESH,
        )

    def far_copy(j):
        return pltpu.make_async_remote_copy(
            src_ref=far_send.at[some(j)],
            dst_ref=far_recv.at[some(j)],
            send_sem=far_send_sem.at[j],
            recv_sem=far_recv_sem.at[j],
            device_id={"ch": far},
            device_id_type=MESH,
        )

    own_side, far_side = lax.div(mine, 2), lax.div(far, 2)

    def turn(j):
        for pair in range(chunk // 2):
            first = j * chunk + 2 * pair
            both = [
                parts[place_ref[2 * k]] + parts[place_ref[2 * k + 1]] for k in (first, first + 1)
            ]
            stack = []
            for t in range(TURNS // 2):
                a, b = (x[:, t * LANES : (t + 1) * LANES] for x in both)
                stack.append(jnp.where(low, a, pltpu.roll(b, LANES // 2, 1)))
                stack.append(jnp.where(low, pltpu.roll(a, LANES // 2, 1), b))
            flat = jnp.concatenate(stack, axis=0).T
            for i in range(2):
                for b in range(STEP):
                    at = (i * STEP + b) * SHIFTS
                    turned[first + i, pl.ds(b, SHIFTS, stride=STEP), :] = flat[at : at + SHIFTS]

    def pass_on(j):
        near_copy(j, far_side).wait_recv()
        far_send[some(j)] = turned[some(j), spots(far)] + near_recv[far_side, some(j)]
        far_copy(j).start()

    def reduce(j, carry):
        turn(j)
        near_copy(j, far_side).start()
        near_copy(j, own_side).start()

        @pl.when(j >= lag)
        def _():
            pass_on(j - lag)

        return carry

    lax.fori_loop(0, chunks, reduce, 0)

    def drain(j, carry):
        pass_on(j)
        return carry

    lax.fori_loop(chunks - lag, chunks, drain, 0)

    def finish(j, carry):
        near_copy(j, own_side).wait_recv()
        far_copy(j).wait_recv()
        value = turned[some(j), spots(mine)] + near_recv[own_side, some(j)] + far_recv[some(j)]
        out_ref[some(j)] = value
        near_copy(j, far_side).wait_send()
        near_copy(j, own_side).wait_send()
        far_copy(j).wait_send()
        return carry

    lax.fori_loop(0, chunks, finish, 0)

    def close(i, carry):
        trace_copy(i).wait_send()
        return carry

    lax.fori_loop(1, blocks, close, 0)


def per_device(waveform, templates, block_of, trace_of):
    me = lax.axis_index("st")
    blocks = lax.axis_size("st")
    own, chans, taps = templates.shape
    half = chans // 2
    stations, comps, window = waveform.shape
    lags = window - taps
    used = window // LANES
    depth = taps + LANES
    pairs = 2 * own
    slots = -(-13 * pairs // (10 * blocks))
    chunk = 4
    assert own % chunk == 0 and lags == 64 * LANES and used % 4 == 0

    sources = lax.dynamic_index_in_dim(block_of[0].reshape(blocks, own, 2), me, 0, keepdims=False)
    named = sources.reshape(pairs)
    ids = jnp.arange(pairs, dtype=jnp.int32)
    earlier = (named[None, :] == named[:, None]) & (ids[None, :] < ids[:, None])
    place = named * slots + jnp.sum(earlier.astype(jnp.int32), axis=1)
    where = jnp.arange(blocks * slots, dtype=jnp.int32)
    order = jnp.sum(jnp.where(place[None, :] == where[:, None], ids[None, :], 0), axis=1)

    wanted = lax.dynamic_index_in_dim(trace_of[0], me, 1, keepdims=False).reshape(-1)
    rows = jnp.arange(stations * comps, dtype=jnp.int32)
    trace = (rows % stations) * comps + rows // stations
    select = (wanted[:, None] == trace[None, :]).astype(BF16)
    wave = jnp.transpose(waveform, (1, 0, 2)).reshape(stations * comps, window)

    spots = np.arange(LANES)
    later = spots[:, None] >= spots[None, :]
    steps = np.concatenate([later, ~later, np.ones_like(later)], axis=1)
    steps = jnp.asarray(np.concatenate([steps, steps], axis=0), BF16)

    dims = (blocks, slots, own, half, taps, used, depth, lags, chunk, 3)
    rows = half * used
    piece = lags // LANES // 4
    smem = pl.BlockSpec(memory_space=pltpu.SMEM)
    vmem = pl.BlockSpec(memory_space=pltpu.VMEM)
    dma = pltpu.SemaphoreType.DMA
    out = pl.pallas_call(
        functools.partial(kernel, dims),
        out_shape=jax.ShapeDtypeStruct((own, piece, LANES), F32),
        in_specs=[smem, smem, vmem, vmem, vmem, vmem],
        out_specs=vmem,
        scratch_shapes=[
            pltpu.VMEM((blocks * rows, LANES), F32),
            pltpu.VMEM((blocks, rows, LANES), BF16),
            pltpu.VMEM((blocks, rows, LANES), BF16),
            pltpu.VMEM((pairs, half, SHIFTS, depth), BF16),
            pltpu.VMEM((pairs, half, LANES), F32),
            pltpu.VMEM((rows + 8, LANES), F32),
            pltpu.VMEM((TURNS - 1, rows + 8, LANES), F32),
            pltpu.VMEM((rows, LANES), F32),
            pltpu.VMEM((rows, LANES), F32),
            pltpu.VMEM((rows, LANES), F32),
            pltpu.VMEM((half, TURNS * TURNS, SHIFTS, LANES), BF16),
            pltpu.VMEM((half, SHIFTS, lags // SHIFTS), F32),
            pltpu.VMEM((blocks * slots, SHIFTS, lags // SHIFTS), F32),
            pltpu.VMEM((own, lags // LANES, LANES), F32),
            pltpu.VMEM((2, own, piece, LANES), F32),
            pltpu.VMEM((own, piece, LANES), F32),
            pltpu.VMEM((own, piece, LANES), F32),
            pltpu.VMEM((8, LANES), F32),
            dma((blocks,)),
            dma((blocks,)),
            dma((own // chunk, 2)),
            dma((own // chunk, 2)),
            dma((own // chunk,)),
            dma((own // chunk,)),
        ],
        compiler_params=pltpu.CompilerParams(
            collective_id=0, has_side_effects=True, vmem_limit_bytes=56 * 1024 * 1024
        ),
        name="detect",
    )(order, place, select, wave, templates, steps)
    return out.reshape(own, -1)


def solution(mesh):
    in_specs = (
        P("st", None, None),
        P("st", "ch", None),
        P("ch", None, None),
        P("ch", None, None, None),
    )
    return jax.shard_map(
        per_device, mesh=mesh, in_specs=in_specs, out_specs=P("st", "ch"), check_vma=False
    )
```

time: 65.6 us -> 44.9 us (0.68)
  waiting for transfers between devices: 24.3 us -> 0 us
  Pallas kernels: 21.1 us -> 39 us
  starting transfers between devices: 8.9 us -> 0 us
  local copies, waits for them, and re-layouts: 10.1 us -> 4.03 us
  other arithmetic: 0.78 us -> 1.58 us
    pallas_call x1, Pallas kernels: 21.1 us -> 39 us  [per_device(): pl.pallas_call(functools.partial(kernel, dims), out_shape=jax.ShapeDtypeS...]
    ppermute x2 -> x0, waiting for transfers between devices: 12.7 us -> none  [swapped(): lax.ppermute(x, axis, [(i, i ^ bit) for i in range(lax.axis_size(axis))])]
    all_to_all x1 -> x0, waiting for transfers between devices: 11.6 us -> none  [per_device(): lax.all_to_all(source_rows.reshape(station_count, half_chans, window), 's...]
    all_to_all x1 -> x0, starting transfers between devices: 7.25 us -> none  [per_device(): lax.all_to_all(source_rows.reshape(station_count, half_chans, window), 's...]
    reshape x4 -> x1, local copies, waits for them, and re-layouts: 3.69 us -> 0.13 us  [per_device(): named = sources.reshape(pairs)]
    gather x1 -> x0, local copies, waits for them, and re-layouts: 2.21 us -> none  [per_device(): source_rows = waveform[station, wanted - 3 * station]]
    ppermute x2 -> x0, starting transfers between devices: 1.65 us -> none  [swapped(): lax.ppermute(x, axis, [(i, i ^ bit) for i in range(lax.axis_size(axis))])]
    unnamed x9 -> x7, local copies, waits for them, and re-layouts: 1.29 us -> 2.77 us
  transfers between devices with their start and end apart: 3 -> 0, of which waited for: 3 -> 0; matrix products, arithmetic and copies ran while one was open for 6% -> 0% of each run, Pallas kernels for 0% -> 0%
where the time goes in v1:
time: 44.9 us; the launch traced here: 44.6 us
  Pallas kernels  39 us (87%)
  local copies, waits for them, and re-layouts  4.03 us (9%)
  other arithmetic  1.58 us (4%)
    pallas_call x1, Pallas kernels, per_device(): pl.pallas_call(functools.partial(kernel, dims), out_shape=jax.ShapeDtypeS...  39 us
    unnamed x7, local copies, waits for them, and re-layouts  2.77 us

profile of v1, /device:TPU:0, one launch (start us, length us, event | category | flops | bytes accessed | tf_op | source)
XLA Modules:
  0.0 44.6 jit_solution(8767860433470074268)
XLA Ops:
  0.0 0.0 copy-start
  0.0 0.7 %copy-done = s32[1,8,8,4]{2,3,1,0:T(4,128)S(1)} copy-done((s32[1,8,8,4]{2,3,1,0:T(4,128)S(1)}, s32[1,8,8,4]{2,3,1,0:T(4,128)}, u32[]{:S(2)}) %copy-start) | copy-done | bytes 1048
  0.7 0.3 dynamic-slice_reduce_fusion
  1.0 0.1 eq.49
  1.1 0.7 %compare_convert_fusion.select_ref = bf16[32,96]{1,0:T(8,128)(2,1)} fusion(s32[96]{0:T(128)S(1)} %fusion.2, s32[32]{0:T(128)S(1)} %eq.49), kind=kLoop, calls=%fused_computation.6 | loop fusion | flops 6144 | bytes 6656 | tf_op jit(solution)/shard_map/convert_element_type | solution.py:341
  1.8 0.8 %reshape_squeeze.3 = s32[8,52,2]{1,0,2:T(8,128)S(1)} reshape(s32[1,416,2]{1,2,0:T(2,128)} %param.7) | data formatting | bytes 6656 | tf_op jit(solution)/shard_map/reshape;squeeze | solution.py:330
  2.5 0.1 copy.9
  2.6 0.1 reshape.48
  2.8 0.2 convert_reduce_fusion
  3.0 0.0 copy-start.1
  3.0 0.7 %select_reduce_fusion.order_ref = s32[136]{0:T(256)} fusion(s32[104]{0:T(128)S(1)} %multiply_add_fusion.place_ref), kind=kLoop, calls=%fused_computation | loop fusion | flops 42296 | bytes 960 | tf_op jit(solution)/shard_map/reduce_sum | solution.py:336
  3.7 0.0 copy-done.1
  3.7 39.0 %detect.1 = f32[52,16,128]{2,1,0:T(8,128)} custom-call(s32[136]{0:T(256)} %select_reduce_fusion.order_ref, s32[104]{0:T(128)} %copy-done.1, bf16[32,96]{1,0:T(8,128)(2,1)} %compare_convert_fusion.select_ref, bf16[96,8704]{1,0:T(8,128)(2,1)} %bitcast.9, bf16[52,8,512]{2,1,0:T(8,128)(2,1)} %filters_ref.1, bf16[256,384]{1,0:T(8,128)(2,1)} %constant.54.clone.steps_ref), custom_call_target="tpu_custom_call" | custom-call | tf_op jit(solution)/shard_map/detect/pallas_call | solution.py:355
  42.7 1.0 %pad = f32[56,16,128]{2,1,0:T(8,128)S(1)} pad(f32[52,16,128]{2,1,0:T(8,128)} %detect.1, f32[]{:T(128)} %constant.59), padding=0_4x0_0x0_0 | pad | bytes 884740
  43.7 0.9 %copy.10 = f32[7,8,16,128]{3,1,2,0:T(8,128)} copy(f32[7,8,16,128]{3,2,1,0:T(8,128)S(1)} %bitcast.8) | data formatting | bytes 917504
  (3 shorter events, 0.0 us)
Async XLA Ops:
  0.0 0.7 %copy-start = (s32[1,8,8,4]{2,3,1,0:T(4,128)S(1)}, s32[1,8,8,4]{2,3,1,0:T(4,128)}, u32[]{:S(2)}) copy-start(s32[1,8,8,4]{2,3,1,0:T(4,128)} %param.8) | copy-start | bytes 3076
  3.0 0.7 %copy-start.1 = (s32[104]{0:T(128)}, s32[104]{0:T(128)S(1)}, u32[]{:S(2)}) copy-start(s32[104]{0:T(128)S(1)} %multiply_add_fusion.place_ref) | copy-start | bytes 1252

commit v2 on v1

--- a/solution.py
+++ b/solution.py
@@ -13,6 +13,9 @@
 LANES = 128
 TURNS = LANES // SHIFTS
 STEP = 4
+HALVES = 64
+MOST = 32767.0
+TINY = 1e-30
 MESH = pl.DeviceIdType.MESH
 F32 = jnp.float32
 BF16 = jnp.bfloat16
@@ -28,13 +31,15 @@
 
 def kernel(
     dims,
-    order_ref,
-    place_ref,
-    select_ref,
+    traces_ref,
+    named_ref,
     wave_ref,
     filters_ref,
     steps_ref,
     out_ref,
+    chosen,
+    tables,
+    table,
     stage,
     send,
     recv,
@@ -52,7 +57,12 @@
     near_recv,
     far_send,
     far_recv,
+    peaks_send,
+    peaks_recv,
     summed,
+    table_sem,
+    peaks_send_sem,
+    peaks_recv_sem,
     send_sem,
     recv_sem,
     near_send_sem,
@@ -78,11 +88,25 @@
     for other in (near, far):
         pl.semaphore_signal(barrier, inc=1, device_id={"ch": other}, device_id_type=MESH)
 
+    comps, stations, _ = wave_ref.shape
+    listed = lax.broadcasted_iota(jnp.int32, (half, stations * comps), 1)
+    listed = lax.rem(listed, stations) * comps + lax.div(listed, stations)
+    column = lax.broadcasted_iota(jnp.int32, (half, blocks), 1)
+
+    def choose(owner, carry):
+        wanted = jnp.where(column == me, traces_ref[owner], 0).astype(F32)
+        wanted = jnp.sum(wanted, axis=1, keepdims=True)
+        chosen[pl.ds(owner * half, half), :] = (wanted == listed.astype(F32)).astype(F32)
+        return carry
+
+    lax.fori_loop(0, blocks, choose, 0)
+    select = chosen[...].astype(BF16)
     wide = 4 * LANES
 
     def gather(i, carry):
         at = pl.ds(pl.multiple_of(i * wide, wide), wide)
-        tile = jnp.dot(select_ref[...], wave_ref[:, at], preferred_element_type=F32)
+        wave = wave_ref[:, :, at].reshape(comps * stations, wide)
+        tile = jnp.dot(select, wave, preferred_element_type=F32)
         for j in range(4):
             spots = pl.ds(i * 4 + j, blocks * half, stride=used)
             stage[spots, :] = tile[:, j * LANES : (j + 1) * LANES]
@@ -113,6 +137,44 @@
         return carry
 
     lax.fori_loop(1, blocks, post, 0)
+
+    names = named_ref[...].astype(F32)
+    every = names.shape[1]
+    names = jnp.concatenate([names, jnp.zeros((6, every), F32)], axis=0).astype(BF16)
+    pair = lax.broadcasted_iota(jnp.int32, (LANES, every), 0)
+    spot = lax.broadcasted_iota(jnp.int32, (LANES, every), 1)
+    by_column, by_row = [], []
+    for h in range(2):
+        own = (pair >= h * HALVES) & (pair < h * HALVES + templates)
+        own = own & (spot == me * templates + pair - h * HALVES)
+        own = own.astype(F32).astype(BF16)
+        contract = (((1,), (1,)), ((), ()))
+        by_column.append(
+            lax.dot_general(own, names, contract, preferred_element_type=F32)[:, h : h + 1]
+        )
+        by_row.append(
+            lax.dot_general(names, own, contract, preferred_element_type=F32)[h : h + 1]
+        )
+    by_column, by_row = by_column[0] + by_column[1], by_row[0] + by_row[1]
+    down = lax.broadcasted_iota(jnp.int32, (LANES, LANES), 0)
+    along = lax.broadcasted_iota(jnp.int32, (LANES, LANES), 1)
+    same = by_column == by_row
+    good_down = lax.rem(down, HALVES) < templates
+    good_along = lax.rem(along, HALVES) < templates
+    ranked = jnp.sum((same & (along < down) & good_along).astype(F32), axis=1, keepdims=True)
+    place = by_column * slots + ranked
+    slot = lax.broadcasted_iota(jnp.int32, (LANES, 2 * LANES), 1).astype(F32)
+    valid = lax.rem(lax.broadcasted_iota(jnp.int32, (LANES, 2 * LANES), 0), HALVES) < templates
+    holds = ((slot == place) & valid).astype(F32).astype(BF16)
+    ids = lax.broadcasted_iota(jnp.int32, (8, LANES), 1).astype(F32).astype(BF16)
+    order = jnp.dot(ids, holds, preferred_element_type=F32)
+    tables[:, : 2 * LANES] = order.astype(jnp.int32)
+    ranked = jnp.sum((same & (down < along) & good_down).astype(F32), axis=0, keepdims=True)
+    place = by_row * slots + ranked
+    tables[:, 2 * LANES :] = jnp.broadcast_to(place, (8, LANES)).astype(jnp.int32)
+    table_copy = pltpu.make_async_copy(tables, table, table_sem)
+    table_copy.start()
+
     recv[me] = staged(me)
 
     def spread(k, carry):
@@ -124,12 +186,13 @@
         for c in range(2 * half):
             wave = jnp.broadcast_to(longer[c : c + 1], (SHIFTS, depth))
             wave = pltpu.roll(wave, 0, 1, stride=1, stride_axis=0)
-            skew[2 * k + c // half, c % half] = wave.astype(BF16)
-        gains[2 * k] = gain[:half]
-        gains[2 * k + 1] = gain[half:]
+            skew[c // half * HALVES + k, c % half] = wave.astype(BF16)
+        gains[k] = gain[:half]
+        gains[HALVES + k] = gain[half:]
         return carry
 
     lax.fori_loop(0, templates, spread, 0)
+    table_copy.wait()
 
     lane = lax.broadcasted_iota(jnp.int32, (SHIFTS, LANES), 1)
     low = lane < LANES // 2
@@ -181,10 +244,14 @@
                 scale[c, :, at] = jnp.where(low, even, pltpu.roll(odd, LANES // 2, 1))
                 scale[c + 1, :, at] = jnp.where(low, pltpu.roll(even, LANES // 2, 1), odd)
 
+    def entry(at, most):
+        return jnp.minimum(jnp.maximum(table[0, at], 0), most)
+
     def products(source):
         base = source * slots
+        chosen_pairs = [entry(base + g, 2 * HALVES - 1) for g in range(slots)]
         for c in range(half):
-            left = jnp.concatenate([skew[order_ref[base + g], c] for g in range(slots)], axis=0)
+            left = jnp.concatenate([skew[p, c] for p in chosen_pairs], axis=0)
             tiles = []
             for m in range(TURNS):
                 for b in range(STEP):
@@ -200,7 +267,7 @@
                 preferred_element_type=F32,
             )
             for g in range(slots):
-                gain = gains[order_ref[base + g], pl.ds(c, 1), :]
+                gain = gains[chosen_pairs[g], pl.ds(c, 1), :]
                 gain = jnp.concatenate([gain] * (lags // SHIFTS // LANES), axis=1)
                 term = raw[g * SHIFTS : (g + 1) * SHIFTS] * (scale[c] * gain)
                 if c == 0:
@@ -257,7 +324,9 @@
         for pair in range(chunk // 2):
             first = j * chunk + 2 * pair
             both = [
-                parts[place_ref[2 * k]] + parts[place_ref[2 * k + 1]] for k in (first, first + 1)
+                parts[entry(2 * LANES + k, blocks * slots - 1)]
+                + parts[entry(2 * LANES + HALVES + k, blocks * slots - 1)]
+                for k in (first, first + 1)
             ]
             stack = []
             for t in range(TURNS // 2):
@@ -270,9 +339,26 @@
                     at = (i * STEP + b) * SHIFTS
                     turned[first + i, pl.ds(b, SHIFTS, stride=STEP), :] = flat[at : at + SHIFTS]
 
+    def peaks_copy():
+        return pltpu.make_async_remote_copy(
+            src_ref=peaks_send,
+            dst_ref=peaks_recv,
+            send_sem=peaks_send_sem,
+            recv_sem=peaks_recv_sem,
+            device_id={"ch": far},
+            device_id_type=MESH,
+        )
+
     def pass_on(j):
         near_copy(j, far_side).wait_recv()
-        far_send[some(j)] = turned[some(j), spots(far)] + near_recv[far_side, some(j)]
+        peaks = peaks_send[...]
+        for i in range(chunk):
+            k = j * chunk + i
+            value = turned[k, spots(far)] + near_recv[far_side, k]
+            peak = jnp.maximum(jnp.max(jnp.abs(value), axis=1, keepdims=True), TINY)
+            far_send[k] = jnp.round(value * (MOST / peak)).astype(jnp.int32).astype(jnp.int16)
+            peaks = jnp.where(lane == k, peak, peaks)
+        peaks_send[...] = peaks
         far_copy(j).start()
 
     def reduce(j, carry):
@@ -286,6 +372,7 @@
 
         return carry
 
+    peaks_send[...] = jnp.zeros((piece, LANES), F32)
     lax.fori_loop(0, chunks, reduce, 0)
 
     def drain(j, carry):
@@ -293,18 +380,40 @@
         return carry
 
     lax.fori_loop(chunks - lag, chunks, drain, 0)
+    peaks_copy().start()
+
+    peaks_copy().wait_recv()
 
     def finish(j, carry):
         near_copy(j, own_side).wait_recv()
         far_copy(j).wait_recv()
-        value = turned[some(j), spots(mine)] + near_recv[own_side, some(j)] + far_recv[some(j)]
-        out_ref[some(j)] = value
+        peaks = peaks_recv[...] * (1.0 / MOST)
+        for i in range(chunk):
+            k = j * chunk + i
+            unit = jnp.sum(jnp.where(lane == k, peaks, 0.0), axis=1, keepdims=True)
+            value = far_recv[k].astype(jnp.int32).astype(F32) * unit
+            value = value + (turned[k, spots(mine)] + near_recv[own_side, k])
+            summed[pl.ds(pl.multiple_of(k * piece, 8), piece), :] = value
         near_copy(j, far_side).wait_send()
         near_copy(j, own_side).wait_send()
         far_copy(j).wait_send()
         return carry
 
     lax.fori_loop(0, chunks, finish, 0)
+    peaks_copy().wait_send()
+
+    def lay(first, count):
+        for r in range(piece):
+            found = summed[pl.ds(first * piece + r, count, stride=piece), :]
+            out_ref[pl.ds(first, count), r * LANES : (r + 1) * LANES] = found
+
+    def lay_eight(i, carry):
+        lay(pl.multiple_of(i * 8, 8), 8)
+        return carry
+
+    lax.fori_loop(0, templates // 8, lay_eight, 0)
+    if templates % 8:
+        lay(templates // 8 * 8, templates % 8)
 
     def close(i, carry):
         trace_copy(i).wait_send()
@@ -327,19 +436,9 @@
     chunk = 4
     assert own % chunk == 0 and lags == 64 * LANES and used % 4 == 0
 
-    sources = lax.dynamic_index_in_dim(block_of[0].reshape(blocks, own, 2), me, 0, keepdims=False)
-    named = sources.reshape(pairs)
-    ids = jnp.arange(pairs, dtype=jnp.int32)
-    earlier = (named[None, :] == named[:, None]) & (ids[None, :] < ids[:, None])
-    place = named * slots + jnp.sum(earlier.astype(jnp.int32), axis=1)
-    where = jnp.arange(blocks * slots, dtype=jnp.int32)
-    order = jnp.sum(jnp.where(place[None, :] == where[:, None], ids[None, :], 0), axis=1)
-
-    wanted = lax.dynamic_index_in_dim(trace_of[0], me, 1, keepdims=False).reshape(-1)
-    rows = jnp.arange(stations * comps, dtype=jnp.int32)
-    trace = (rows % stations) * comps + rows // stations
-    select = (wanted[:, None] == trace[None, :]).astype(BF16)
-    wave = jnp.transpose(waveform, (1, 0, 2)).reshape(stations * comps, window)
+    wave = jnp.transpose(waveform, (1, 0, 2))
+    traces = jnp.transpose(trace_of[0], (0, 2, 1))
+    named = jnp.transpose(block_of[0], (1, 0))
 
     spots = np.arange(LANES)
     later = spots[:, None] >= spots[None, :]
@@ -354,15 +453,18 @@
     dma = pltpu.SemaphoreType.DMA
     out = pl.pallas_call(
         functools.partial(kernel, dims),
-        out_shape=jax.ShapeDtypeStruct((own, piece, LANES), F32),
-        in_specs=[smem, smem, vmem, vmem, vmem, vmem],
+        out_shape=jax.ShapeDtypeStruct((own, piece * LANES), F32),
+        in_specs=[vmem] * 5,
         out_specs=vmem,
         scratch_shapes=[
+            pltpu.VMEM((blocks * half, stations * comps), F32),
+            pltpu.VMEM((8, 3 * LANES), jnp.int32),
+            pltpu.SMEM((8, 3 * LANES), jnp.int32),
             pltpu.VMEM((blocks * rows, LANES), F32),
             pltpu.VMEM((blocks, rows, LANES), BF16),
             pltpu.VMEM((blocks, rows, LANES), BF16),
-            pltpu.VMEM((pairs, half, SHIFTS, depth), BF16),
-            pltpu.VMEM((pairs, half, LANES), F32),
+            pltpu.VMEM((2 * HALVES, half, SHIFTS, depth), BF16),
+            pltpu.VMEM((2 * HALVES, half, LANES), F32),
             pltpu.VMEM((rows + 8, LANES), F32),
             pltpu.VMEM((TURNS - 1, rows + 8, LANES), F32),
             pltpu.VMEM((rows, LANES), F32),
@@ -373,9 +475,14 @@
             pltpu.VMEM((blocks * slots, SHIFTS, lags // SHIFTS), F32),
             pltpu.VMEM((own, lags // LANES, LANES), F32),
             pltpu.VMEM((2, own, piece, LANES), F32),
-            pltpu.VMEM((own, piece, LANES), F32),
-            pltpu.VMEM((own, piece, LANES), F32),
-            pltpu.VMEM((8, LANES), F32),
+            pltpu.VMEM((own, piece, LANES), jnp.int16),
+            pltpu.VMEM((own, piece, LANES), jnp.int16),
+            pltpu.VMEM((piece, LANES), F32),
+            pltpu.VMEM((piece, LANES), F32),
+            pltpu.VMEM((own * piece, LANES), F32),
+            dma,
+            dma,
+            dma,
             dma((blocks,)),
             dma((blocks,)),
             dma((own // chunk, 2)),
@@ -387,8 +494,8 @@
             collective_id=0, has_side_effects=True, vmem_limit_bytes=56 * 1024 * 1024
         ),
         name="detect",
-    )(order, place, select, wave, templates, steps)
-    return out.reshape(own, -1)
+    )(traces, named, wave, templates, steps)
+    return out
 
 
 def solution(mesh):

time: 44.9 us -> 38.7 us (0.86)
  Pallas kernels: 39 us -> 36.7 us
  local copies, waits for them, and re-layouts: 4.03 us -> 1.82 us
  other arithmetic: 1.58 us -> 0 us
    pallas_call x1, Pallas kernels: 39 us -> 36.7 us  [per_device(): pl.pallas_call(functools.partial(kernel, dims), out_shape=jax.ShapeDtypeS...]
    unnamed x7 -> x1, local copies, waits for them, and re-layouts: 2.77 us -> 1.82 us
    reduce_sum x2 -> x0, other arithmetic: 0.89 us -> none  [the longest x1 0.71 us: per_device(): jnp.sum(jnp.where(place[None, :] == where[:, None], ids[None, :], 0), axi...]
    another operation x1 -> x0, local copies, waits for them, and re-layouts: 0.76 us -> none  [per_device(): block_of[0].reshape(blocks, own, 2)]
    convert_element_type x1 -> x0, other arithmetic: 0.69 us -> none  [per_device(): select = (wanted[:, None] == trace[None, :]).astype(BF16)]
where the time goes in v2:
time: 38.7 us; the launch traced here: 38.6 us
  Pallas kernels  36.7 us (95%)
  local copies, waits for them, and re-layouts  1.82 us (5%)
    pallas_call x1, Pallas kernels, per_device(): pl.pallas_call(functools.partial(kernel, dims), out_shape=jax.ShapeDtypeS...  36.7 us
    unnamed x1, local copies, waits for them, and re-layouts  1.82 us

profile of v2, /device:TPU:0, one launch (start us, length us, event | category | flops | bytes accessed | tf_op | source)
XLA Modules:
  0.0 38.6 jit_solution(14410848593597650912)
XLA Ops:
  0.0 36.7 %detect.1 = f32[52,2048]{1,0:T(8,128)} custom-call(s32[8,4,8]{2,1,0:T(4,128)} %bitcast.8, s32[2,416]{1,0:T(2,128)} %bitcast.9, bf16[3,32,8704]{2,1,0:T(8,128)(2,1)} %bitcast.7, bf16[52,8,512]{2,1,0:T(8,128)(2,1)} %filters_ref.1, bf16[256,384]{1,0:T(8,128)(2,1)} %constant.2.clone.steps_ref), custom_call_target="tpu_custom_call" | custom-call | tf_op jit(solution)/shard_map/detect/pallas_call | solution.py:454
  36.8 1.8 %copy.7 = f32[52,2048]{1,0:T(8,128)} copy(f32[52,2048]{1,0:T(8,128)} %detect.1) | data formatting | bytes 851968

commit v3 on v2

--- a/solution.py
+++ b/solution.py
@@ -31,12 +31,18 @@
 
 def kernel(
     dims,
+    traces_hbm,
+    named_hbm,
+    wave_hbm,
+    filters_hbm,
+    steps_hbm,
+    near_ref,
+    far_ref,
     traces_ref,
     named_ref,
     wave_ref,
     filters_ref,
     steps_ref,
-    out_ref,
     chosen,
     tables,
     table,
@@ -60,6 +66,7 @@
     peaks_send,
     peaks_recv,
     summed,
+    load_sem,
     table_sem,
     peaks_send_sem,
     peaks_recv_sem,
@@ -70,11 +77,33 @@
     far_send_sem,
     far_recv_sem,
 ):
-    blocks, slots, templates, half, taps, used, depth, lags, chunk, lag = dims
+    blocks, slots, templates, half, taps, used, depth, lags, bounds = dims
     me = lax.axis_index("st")
     mine = lax.axis_index("ch")
     near, far = flipped(mine, 1, 4), flipped(mine, 2, 4)
     rows = half * used
+    window = used * LANES
+    parcels = [(a * window // 4, window // 4) for a in range(4)]
+    waves = [
+        pltpu.make_async_copy(
+            wave_hbm.at[:, :, pl.ds(*at)], wave_ref.at[:, :, pl.ds(*at)], load_sem.at[4 + a]
+        )
+        for a, at in enumerate(parcels)
+    ]
+    others = [
+        pltpu.make_async_copy(held, target, load_sem.at[a])
+        for a, (held, target) in enumerate(
+            (
+                (traces_hbm, traces_ref),
+                (named_hbm, named_ref),
+                (filters_hbm, filters_ref),
+                (steps_hbm, steps_ref),
+            )
+        )
+    ]
+    others[0].start()
+    for copy in waves + others[1:]:
+        copy.start()
 
     barrier = pltpu.get_barrier_semaphore()
 
@@ -99,20 +128,21 @@
         chosen[pl.ds(owner * half, half), :] = (wanted == listed.astype(F32)).astype(F32)
         return carry
 
+    others[0].wait()
     lax.fori_loop(0, blocks, choose, 0)
     select = chosen[...].astype(BF16)
-    wide = 4 * LANES
+    wide = LANES
 
     def gather(i, carry):
         at = pl.ds(pl.multiple_of(i * wide, wide), wide)
         wave = wave_ref[:, :, at].reshape(comps * stations, wide)
         tile = jnp.dot(select, wave, preferred_element_type=F32)
-        for j in range(4):
-            spots = pl.ds(i * 4 + j, blocks * half, stride=used)
-            stage[spots, :] = tile[:, j * LANES : (j + 1) * LANES]
-        return carry
-
-    lax.fori_loop(0, used * LANES // wide, gather, 0)
+        stage[pl.ds(i, blocks * half, stride=used), :] = tile
+        return carry
+
+    for a, copy in enumerate(waves):
+        copy.wait()
+        lax.fori_loop(a * used // 4, (a + 1) * used // 4, gather, 0, unroll=True)
 
     def staged(block):
         return stage[pl.ds(pl.multiple_of(block * rows, 16), rows), :].astype(BF16)
@@ -136,8 +166,11 @@
         trace_copy(i).start()
         return carry
 
-    lax.fori_loop(1, blocks, post, 0)
-
+    first_wave = blocks * 3 // 4
+    lax.fori_loop(1, first_wave, post, 0)
+
+    for copy in others[1:]:
+        copy.wait()
     names = named_ref[...].astype(F32)
     every = names.shape[1]
     names = jnp.concatenate([names, jnp.zeros((6, every), F32)], axis=0).astype(BF16)
@@ -275,8 +308,17 @@
                 else:
                     parts[base + g] += term
 
+    def close(i, carry):
+        trace_copy(i).wait_send()
+        return carry
+
     def work(i, carry):
         source = flipped(me, i, blocks)
+
+        @pl.when(i == 2)
+        def _():
+            lax.fori_loop(blocks // 2, first_wave, close, 0)
+            lax.fori_loop(first_wave, blocks, post, 0)
 
         @pl.when(i > 0)
         def _():
@@ -289,10 +331,10 @@
     lax.fori_loop(0, blocks, work, 0)
 
     piece = lags // LANES // 4
-    chunks = templates // chunk
+    own_side, far_side = lax.div(mine, 2), lax.div(far, 2)
 
     def some(j):
-        return pl.ds(j * chunk, chunk)
+        return pl.ds(bounds[j], bounds[j + 1] - bounds[j])
 
     def spots(number):
         return pl.ds(pl.multiple_of(number * piece, 8), piece)
@@ -318,108 +360,81 @@
             device_id_type=MESH,
         )
 
-    own_side, far_side = lax.div(mine, 2), lax.div(far, 2)
-
-    def turn(j):
-        for pair in range(chunk // 2):
-            first = j * chunk + 2 * pair
-            both = [
+    def peaks_copy(j):
+        return pltpu.make_async_remote_copy(
+            src_ref=peaks_send.at[j],
+            dst_ref=peaks_recv.at[j],
+            send_sem=peaks_send_sem.at[j],
+            recv_sem=peaks_recv_sem.at[j],
+            device_id={"ch": far},
+            device_id_type=MESH,
+        )
+
+    def turn(j, carry):
+        both = []
+        for i in range(2):
+            k = 2 * j + i
+            both.append(
                 parts[entry(2 * LANES + k, blocks * slots - 1)]
                 + parts[entry(2 * LANES + HALVES + k, blocks * slots - 1)]
-                for k in (first, first + 1)
-            ]
-            stack = []
-            for t in range(TURNS // 2):
-                a, b = (x[:, t * LANES : (t + 1) * LANES] for x in both)
-                stack.append(jnp.where(low, a, pltpu.roll(b, LANES // 2, 1)))
-                stack.append(jnp.where(low, pltpu.roll(a, LANES // 2, 1), b))
-            flat = jnp.concatenate(stack, axis=0).T
-            for i in range(2):
-                for b in range(STEP):
-                    at = (i * STEP + b) * SHIFTS
-                    turned[first + i, pl.ds(b, SHIFTS, stride=STEP), :] = flat[at : at + SHIFTS]
-
-    def peaks_copy():
-        return pltpu.make_async_remote_copy(
-            src_ref=peaks_send,
-            dst_ref=peaks_recv,
-            send_sem=peaks_send_sem,
-            recv_sem=peaks_recv_sem,
-            device_id={"ch": far},
-            device_id_type=MESH,
-        )
+            )
+        stack = []
+        for t in range(TURNS // 2):
+            a, b = (x[:, t * LANES : (t + 1) * LANES] for x in both)
+            stack.append(jnp.where(low, a, pltpu.roll(b, LANES // 2, 1)))
+            stack.append(jnp.where(low, pltpu.roll(a, LANES // 2, 1), b))
+        flat = jnp.concatenate(stack, axis=0).T
+        for i in range(2):
+            for b in range(STEP):
+                at = (i * STEP + b) * SHIFTS
+                turned[2 * j + i, pl.ds(b, SHIFTS, stride=STEP), :] = flat[at : at + SHIFTS]
+        return carry
 
     def pass_on(j):
         near_copy(j, far_side).wait_recv()
-        peaks = peaks_send[...]
-        for i in range(chunk):
-            k = j * chunk + i
-            value = turned[k, spots(far)] + near_recv[far_side, k]
-            peak = jnp.maximum(jnp.max(jnp.abs(value), axis=1, keepdims=True), TINY)
-            far_send[k] = jnp.round(value * (MOST / peak)).astype(jnp.int32).astype(jnp.int16)
-            peaks = jnp.where(lane == k, peak, peaks)
-        peaks_send[...] = peaks
+        value = turned[some(j), spots(far)] + near_recv[far_side, some(j)]
+        tiles = value.reshape(-1, 8, LANES)
+        peak = jnp.maximum(jnp.max(jnp.abs(tiles), axis=0), TINY)
+        peaks_send[j] = peak
+        peaks_copy(j).start()
+        whole = jnp.round(tiles * (MOST / peak)[None]).astype(jnp.int32)
+        far_send[some(j)] = whole.reshape(value.shape).astype(jnp.int16)
         far_copy(j).start()
 
-    def reduce(j, carry):
-        turn(j)
+    def lay(target, j, value):
+        first, count = bounds[j], bounds[j + 1] - bounds[j]
+        summed[: count * piece, :] = value.reshape(count * piece, LANES)
+        for k in range(0, count, 8):
+            size = min(8, count - k)
+            for r in range(piece):
+                found = summed[pl.ds(k * piece + r, size, stride=piece), :]
+                target[first + k : first + k + size, r * LANES : (r + 1) * LANES] = found
+
+    pieces = len(bounds) - 1
+    for j in range(pieces):
+        lax.fori_loop(bounds[j] // 2, bounds[j + 1] // 2, turn, 0, unroll=2)
         near_copy(j, far_side).start()
         near_copy(j, own_side).start()
-
-        @pl.when(j >= lag)
-        def _():
-            pass_on(j - lag)
-
-        return carry
-
-    peaks_send[...] = jnp.zeros((piece, LANES), F32)
-    lax.fori_loop(0, chunks, reduce, 0)
-
-    def drain(j, carry):
-        pass_on(j)
-        return carry
-
-    lax.fori_loop(chunks - lag, chunks, drain, 0)
-    peaks_copy().start()
-
-    peaks_copy().wait_recv()
-
-    def finish(j, carry):
+        if j > 0:
+            pass_on(j - 1)
+    pass_on(pieces - 1)
+    for j in range(pieces):
         near_copy(j, own_side).wait_recv()
+        lay(near_ref, j, turned[some(j), spots(mine)] + near_recv[own_side, some(j)])
+    for j in range(pieces):
+        peaks_copy(j).wait_recv()
         far_copy(j).wait_recv()
-        peaks = peaks_recv[...] * (1.0 / MOST)
-        for i in range(chunk):
-            k = j * chunk + i
-            unit = jnp.sum(jnp.where(lane == k, peaks, 0.0), axis=1, keepdims=True)
-            value = far_recv[k].astype(jnp.int32).astype(F32) * unit
-            value = value + (turned[k, spots(mine)] + near_recv[own_side, k])
-            summed[pl.ds(pl.multiple_of(k * piece, 8), piece), :] = value
+        whole = far_recv[some(j)].astype(jnp.int32).astype(F32)
+        tiles = whole.reshape(-1, 8, LANES) * (peaks_recv[j] * (1.0 / MOST))[None]
+        lay(far_ref, j, tiles)
+    for j in range(pieces):
         near_copy(j, far_side).wait_send()
         near_copy(j, own_side).wait_send()
         far_copy(j).wait_send()
-        return carry
-
-    lax.fori_loop(0, chunks, finish, 0)
-    peaks_copy().wait_send()
-
-    def lay(first, count):
-        for r in range(piece):
-            found = summed[pl.ds(first * piece + r, count, stride=piece), :]
-            out_ref[pl.ds(first, count), r * LANES : (r + 1) * LANES] = found
-
-    def lay_eight(i, carry):
-        lay(pl.multiple_of(i * 8, 8), 8)
-        return carry
-
-    lax.fori_loop(0, templates // 8, lay_eight, 0)
-    if templates % 8:
-        lay(templates // 8 * 8, templates % 8)
-
-    def close(i, carry):
-        trace_copy(i).wait_send()
-        return carry
-
-    lax.fori_loop(1, blocks, close, 0)
+        peaks_copy(j).wait_send()
+
+    lax.fori_loop(1, blocks // 2, close, 0)
+    lax.fori_loop(first_wave, blocks, close, 0)
 
 
 def per_device(waveform, templates, block_of, trace_of):
@@ -433,8 +448,9 @@
     depth = taps + LANES
     pairs = 2 * own
     slots = -(-13 * pairs // (10 * blocks))
-    chunk = 4
-    assert own % chunk == 0 and lags == 64 * LANES and used % 4 == 0
+    bounds = (0, 8, 24, 40, own)
+    count = len(bounds) - 1
+    assert 40 < own <= HALVES and own % 2 == 0 and lags == 64 * LANES and used % 4 == 0
 
     wave = jnp.transpose(waveform, (1, 0, 2))
     traces = jnp.transpose(trace_of[0], (0, 2, 1))
@@ -445,18 +461,25 @@
     steps = np.concatenate([later, ~later, np.ones_like(later)], axis=1)
     steps = jnp.asarray(np.concatenate([steps, steps], axis=0), BF16)
 
-    dims = (blocks, slots, own, half, taps, used, depth, lags, chunk, 3)
+    dims = (blocks, slots, own, half, taps, used, depth, lags, bounds)
     rows = half * used
     piece = lags // LANES // 4
     smem = pl.BlockSpec(memory_space=pltpu.SMEM)
     vmem = pl.BlockSpec(memory_space=pltpu.VMEM)
     dma = pltpu.SemaphoreType.DMA
-    out = pl.pallas_call(
+    given = (traces, named, wave, templates, steps)
+    given = [pltpu.with_memory_space_constraint(x, pltpu.HBM) for x in given]
+    near, far = pl.pallas_call(
         functools.partial(kernel, dims),
-        out_shape=jax.ShapeDtypeStruct((own, piece * LANES), F32),
-        in_specs=[vmem] * 5,
-        out_specs=vmem,
+        out_shape=[pltpu.VMEM((own, piece * LANES), F32)] * 2,
+        in_specs=[pl.BlockSpec(memory_space=pltpu.HBM)] * 5,
+        out_specs=[vmem, vmem],
         scratch_shapes=[
+            pltpu.VMEM(traces.shape, jnp.int32),
+            pltpu.VMEM(named.shape, jnp.int32),
+            pltpu.VMEM(wave.shape, BF16),
+            pltpu.VMEM(templates.shape, BF16),
+            pltpu.VMEM(steps.shape, BF16),
             pltpu.VMEM((blocks * half, stations * comps), F32),
             pltpu.VMEM((8, 3 * LANES), jnp.int32),
             pltpu.SMEM((8, 3 * LANES), jnp.int32),
@@ -477,25 +500,26 @@
             pltpu.VMEM((2, own, piece, LANES), F32),
             pltpu.VMEM((own, piece, LANES), jnp.int16),
             pltpu.VMEM((own, piece, LANES), jnp.int16),
-            pltpu.VMEM((piece, LANES), F32),
-            pltpu.VMEM((piece, LANES), F32),
-            pltpu.VMEM((own * piece, LANES), F32),
+            pltpu.VMEM((count, 8, LANES), F32),
+            pltpu.VMEM((count, 8, LANES), F32),
+            pltpu.VMEM((16 * piece, LANES), F32),
+            dma((8,)),
             dma,
-            dma,
-            dma,
+            dma((count,)),
+            dma((count,)),
             dma((blocks,)),
             dma((blocks,)),
-            dma((own // chunk, 2)),
-            dma((own // chunk, 2)),
-            dma((own // chunk,)),
-            dma((own // chunk,)),
+            dma((count, 2)),
+            dma((count, 2)),
+            dma((count,)),
+            dma((count,)),
         ],
         compiler_params=pltpu.CompilerParams(
-            collective_id=0, has_side_effects=True, vmem_limit_bytes=56 * 1024 * 1024
+            collective_id=0, has_side_effects=True, vmem_limit_bytes=(52 + blocks) * 512 * 1024
         ),
         name="detect",
-    )(traces, named, wave, templates, steps)
-    return out
+    )(*given)
+    return near + far
 
 
 def solution(mesh):

time: 38.7 us -> 34.1 us (0.88)
  Pallas kernels: 36.7 us -> 33 us
  local copies, waits for them, and re-layouts: 1.82 us -> 0 us
  other arithmetic: 0 us -> 0.82 us
    pallas_call x1, Pallas kernels: 36.7 us -> 33 us  [per_device(): pl.pallas_call(functools.partial(kernel, dims), out_shape=[pltpu.VMEM((ow...]
    unnamed x1 -> x0, local copies, waits for them, and re-layouts: 1.82 us -> none
    add x0 -> x1, other arithmetic: none -> 0.82 us  [per_device(): return near + far]
where the time goes in v3:
time: 34.1 us; the launch traced here: 33.8 us
  Pallas kernels  33 us (97%)
  other arithmetic  0.82 us (2%)
    pallas_call x1, Pallas kernels, per_device(): pl.pallas_call(functools.partial(kernel, dims), out_shape=[pltpu.VMEM((ow...  33 us
    add x1, other arithmetic, per_device(): return near + far  0.82 us

profile of v3, /device:TPU:0, one launch (start us, length us, event | category | flops | bytes accessed | tf_op | source)
XLA Modules:
  0.0 33.8 jit_solution(11479066499436407425)
XLA Ops:
  0.0 33.0 %detect.1 = (f32[52,2048]{1,0:T(8,128)S(1)}, f32[52,2048]{1,0:T(8,128)S(1)}) custom-call(s32[8,4,8]{2,1,0:T(4,128)} %bitcast.8, s32[2,416]{1,0:T(2,128)} %bitcast.9, bf16[3,32,8704]{2,1,0:T(8,128)(2,1)} %bitcast.7, bf16[52,8,512]{2,1,0:T(8,128)(2,1)} %filters_hbm.1, bf16[256,384]{1,0:T(8,128)(2,1)} %constant.2.clone.steps_hbm), custom_call_target="tpu_custom_call" | custom-call | tf_op jit(solution)/shard_map/detect/pallas_call | solution.py:472
  33.0 0.8 %add.3 = f32[52,2048]{1,0:T(8,128)} add(f32[52,2048]{1,0:T(8,128)S(1)} %get-tuple-element.7, f32[52,2048]{1,0:T(8,128)S(1)} %get-tuple-element.8) | non-fusion elementwise | flops 106496 | bytes 1277952 | tf_op jit(solution)/shard_map/add | solution.py:522

commit v4 on v3

--- a/solution.py
+++ b/solution.py
@@ -14,6 +14,7 @@
 TURNS = LANES // SHIFTS
 STEP = 4
 HALVES = 64
+UNROLL = 4
 MOST = 32767.0
 TINY = 1e-30
 MESH = pl.DeviceIdType.MESH
@@ -210,21 +211,44 @@
 
     recv[me] = staged(me)
 
+    apart = lax.broadcasted_iota(jnp.int32, (SHIFTS, LANES), 1) >= lax.broadcasted_iota(
+        jnp.int32, (SHIFTS, LANES), 0
+    )
+
     def spread(k, carry):
         taken = filters_ref[k].astype(F32)
-        mean = jnp.sum(taken * taken, axis=1, keepdims=True) / taps
-        gain = 1.0 / (taps * jnp.sqrt(mean + EPSILON))
-        gain = jnp.broadcast_to(gain, (2 * half, LANES))
-        longer = jnp.concatenate([taken, jnp.zeros((2 * half, depth - taps), F32)], axis=1)
         for c in range(2 * half):
-            wave = jnp.broadcast_to(longer[c : c + 1], (SHIFTS, depth))
-            wave = pltpu.roll(wave, 0, 1, stride=1, stride_axis=0)
-            skew[c // half * HALVES + k, c % half] = wave.astype(BF16)
-        gains[k] = gain[:half]
-        gains[HALVES + k] = gain[half:]
-        return carry
-
-    lax.fori_loop(0, templates, spread, 0)
+            past = jnp.zeros((SHIFTS, LANES), F32)
+            for q in range(taps // LANES + 1):
+                if q < taps // LANES:
+                    tile = taken[c : c + 1, q * LANES : (q + 1) * LANES]
+                    tile = jnp.broadcast_to(tile, (SHIFTS, LANES))
+                    tile = pltpu.roll(tile, 0, 1, stride=1, stride_axis=0)
+                else:
+                    tile = jnp.zeros((SHIFTS, LANES), F32)
+                at = slice(q * LANES, (q + 1) * LANES)
+                skew[c // half * HALVES + k, c % half, :, at] = jnp.where(
+                    apart, tile, past
+                ).astype(BF16)
+                past = tile
+        return carry
+
+    lax.fori_loop(0, templates, spread, 0, unroll=UNROLL)
+
+    batch = templates // 4
+
+    def weigh(j, carry):
+        for i in range(batch):
+            k = j * batch + i
+            taken = filters_ref[k].astype(F32)
+            mean = jnp.sum(taken * taken, axis=1, keepdims=True) / taps
+            gain = 1.0 / (taps * jnp.sqrt(mean + EPSILON))
+            gain = jnp.broadcast_to(gain, (2 * half, LANES))
+            gains[k] = gain[:half]
+            gains[HALVES + k] = gain[half:]
+        return carry
+
+    lax.fori_loop(0, 4, weigh, 0)
     table_copy.wait()
 
     lane = lax.broadcasted_iota(jnp.int32, (SHIFTS, LANES), 1)
@@ -412,7 +436,7 @@
 
     pieces = len(bounds) - 1
     for j in range(pieces):
-        lax.fori_loop(bounds[j] // 2, bounds[j + 1] // 2, turn, 0, unroll=2)
+        lax.fori_loop(bounds[j] // 2, bounds[j + 1] // 2, turn, 0, unroll=4)
         near_copy(j, far_side).start()
         near_copy(j, own_side).start()
         if j > 0:
@@ -450,7 +474,7 @@
     slots = -(-13 * pairs // (10 * blocks))
     bounds = (0, 8, 24, 40, own)
     count = len(bounds) - 1
-    assert 40 < own <= HALVES and own % 2 == 0 and lags == 64 * LANES and used % 4 == 0
+    assert 40 < own <= HALVES and own % 4 == 0 and lags == 64 * LANES and used % 4 == 0
 
     wave = jnp.transpose(waveform, (1, 0, 2))
     traces = jnp.transpose(trace_of[0], (0, 2, 1))

time: 34.1 us -> 30.4 us (0.89)
  Pallas kernels: 33 us -> 29.4 us
    pallas_call x1, Pallas kernels: 33 us -> 29.4 us  [per_device(): pl.pallas_call(functools.partial(kernel, dims), out_shape=[pltpu.VMEM((ow...]
where the time goes in v4:
time: 30.4 us; the launch traced here: 30.2 us
  Pallas kernels  29.4 us (97%)
  other arithmetic  0.82 us (3%)
    pallas_call x1, Pallas kernels, per_device(): pl.pallas_call(functools.partial(kernel, dims), out_shape=[pltpu.VMEM((ow...  29.4 us
    add x1, other arithmetic, per_device(): return near + far  0.82 us

profile of v4, /device:TPU:0, one launch (start us, length us, event | category | flops | bytes accessed | tf_op | source)
XLA Modules:
  0.0 30.2 jit_solution(15405139945701126411)
XLA Ops:
  0.0 29.4 %detect.1 = (f32[52,2048]{1,0:T(8,128)S(1)}, f32[52,2048]{1,0:T(8,128)S(1)}) custom-call(s32[8,4,8]{2,1,0:T(4,128)} %bitcast.8, s32[2,416]{1,0:T(2,128)} %bitcast.9, bf16[3,32,8704]{2,1,0:T(8,128)(2,1)} %bitcast.7, bf16[52,8,512]{2,1,0:T(8,128)(2,1)} %filters_hbm.1, bf16[256,384]{1,0:T(8,128)(2,1)} %constant.2.clone.steps_hbm), custom_call_target="tpu_custom_call" | custom-call | tf_op jit(solution)/shard_map/detect/pallas_call | solution.py:496
  29.4 0.8 %add.3 = f32[52,2048]{1,0:T(8,128)} add(f32[52,2048]{1,0:T(8,128)S(1)} %get-tuple-element.7, f32[52,2048]{1,0:T(8,128)S(1)} %get-tuple-element.8) | non-fusion elementwise | flops 106496 | bytes 1277952 | tf_op jit(solution)/shard_map/add | solution.py:546

commit v5 on v4

--- a/solution.py
+++ b/solution.py
@@ -14,7 +14,7 @@
 TURNS = LANES // SHIFTS
 STEP = 4
 HALVES = 64
-UNROLL = 4
+UNROLL = 13
 MOST = 32767.0
 TINY = 1e-30
 MESH = pl.DeviceIdType.MESH
@@ -84,7 +84,7 @@
     near, far = flipped(mine, 1, 4), flipped(mine, 2, 4)
     rows = half * used
     window = used * LANES
-    parcels = [(a * window // 4, window // 4) for a in range(4)]
+    parcels = [(0, window)]
     waves = [
         pltpu.make_async_copy(
             wave_hbm.at[:, :, pl.ds(*at)], wave_ref.at[:, :, pl.ds(*at)], load_sem.at[4 + a]
@@ -130,20 +130,18 @@
         return carry
 
     others[0].wait()
-    lax.fori_loop(0, blocks, choose, 0)
+    lax.fori_loop(0, blocks, choose, 0, unroll=8)
     select = chosen[...].astype(BF16)
-    wide = LANES
-
-    def gather(i, carry):
-        at = pl.ds(pl.multiple_of(i * wide, wide), wide)
-        wave = wave_ref[:, :, at].reshape(comps * stations, wide)
-        tile = jnp.dot(select, wave, preferred_element_type=F32)
-        stage[pl.ds(i, blocks * half, stride=used), :] = tile
-        return carry
-
     for a, copy in enumerate(waves):
         copy.wait()
-        lax.fori_loop(a * used // 4, (a + 1) * used // 4, gather, 0, unroll=True)
+        begin, size = parcels[a]
+        each = size // 1
+        for piece_at in range(begin, begin + size, each):
+            wave = wave_ref[:, :, piece_at : piece_at + each].reshape(comps * stations, each)
+            tile = jnp.dot(select, wave, preferred_element_type=F32)
+            for j in range(each // LANES):
+                rows_at = pl.ds(piece_at // LANES + j, blocks * half, stride=used)
+                stage[rows_at, :] = tile[:, j * LANES : (j + 1) * LANES]
 
     def staged(block):
         return stage[pl.ds(pl.multiple_of(block * rows, 16), rows), :].astype(BF16)

time: 30.4 us -> 29.8 us (0.980)
  Pallas kernels: 29.4 us -> 28.8 us
    pallas_call x1, Pallas kernels: 29.4 us -> 28.8 us  [per_device(): pl.pallas_call(functools.partial(kernel, dims), out_shape=[pltpu.VMEM((ow...]
where the time goes in v5:
time: 29.8 us; the launch traced here: 29.6 us
  Pallas kernels  28.8 us (97%)
  other arithmetic  0.82 us (3%)
    pallas_call x1, Pallas kernels, per_device(): pl.pallas_call(functools.partial(kernel, dims), out_shape=[pltpu.VMEM((ow...  28.8 us
    add x1, other arithmetic, per_device(): return near + far  0.82 us

profile of v5, /device:TPU:0, one launch (start us, length us, event | category | flops | bytes accessed | tf_op | source)
XLA Modules:
  0.0 29.6 jit_solution(11495014578531656357)
XLA Ops:
  0.0 28.8 %detect.1 = (f32[52,2048]{1,0:T(8,128)S(1)}, f32[52,2048]{1,0:T(8,128)S(1)}) custom-call(s32[8,4,8]{2,1,0:T(4,128)} %bitcast.8, s32[2,416]{1,0:T(2,128)} %bitcast.9, bf16[3,32,8704]{2,1,0:T(8,128)(2,1)} %bitcast.7, bf16[52,8,512]{2,1,0:T(8,128)(2,1)} %filters_hbm.1, bf16[256,384]{1,0:T(8,128)(2,1)} %constant.2.clone.steps_hbm), custom_call_target="tpu_custom_call" | custom-call | tf_op jit(solution)/shard_map/detect/pallas_call | solution.py:494
  28.8 0.8 %add.3 = f32[52,2048]{1,0:T(8,128)} add(f32[52,2048]{1,0:T(8,128)S(1)} %get-tuple-element.7, f32[52,2048]{1,0:T(8,128)S(1)} %get-tuple-element.8) | non-fusion elementwise | flops 106496 | bytes 1277952 | tf_op jit(solution)/shard_map/add | solution.py:544

commit v6 on v5

--- a/solution.py
+++ b/solution.py
@@ -166,7 +166,7 @@
         return carry
 
     first_wave = blocks * 3 // 4
-    lax.fori_loop(1, first_wave, post, 0)
+    lax.fori_loop(1, first_wave, post, 0, unroll=True)
 
     for copy in others[1:]:
         copy.wait()
@@ -436,10 +436,11 @@
     for j in range(pieces):
         lax.fori_loop(bounds[j] // 2, bounds[j + 1] // 2, turn, 0, unroll=4)
         near_copy(j, far_side).start()
-        near_copy(j, own_side).start()
         if j > 0:
             pass_on(j - 1)
+            near_copy(j - 1, own_side).start()
     pass_on(pieces - 1)
+    near_copy(pieces - 1, own_side).start()
     for j in range(pieces):
         near_copy(j, own_side).wait_recv()
         lay(near_ref, j, turned[some(j), spots(mine)] + near_recv[own_side, some(j)])

time: 29.8 us -> 29.8 us (level)
  no operation moved by 1% of the time
where the time goes in v6:
time: 29.8 us; the launch traced here: 29.6 us
  Pallas kernels  28.8 us (97%)
  other arithmetic  0.82 us (3%)
    pallas_call x1, Pallas kernels, per_device(): pl.pallas_call(functools.partial(kernel, dims), out_shape=[pltpu.VMEM((ow...  28.8 us
    add x1, other arithmetic, per_device(): return near + far  0.82 us

profile of v6, /device:TPU:0, one launch (start us, length us, event | category | flops | bytes accessed | tf_op | source)
XLA Modules:
  0.0 29.6 jit_solution(14310171847596833934)
XLA Ops:
  0.0 28.8 %detect.1 = (f32[52,2048]{1,0:T(8,128)S(1)}, f32[52,2048]{1,0:T(8,128)S(1)}) custom-call(s32[8,4,8]{2,1,0:T(4,128)} %bitcast.8, s32[2,416]{1,0:T(2,128)} %bitcast.9, bf16[3,32,8704]{2,1,0:T(8,128)(2,1)} %bitcast.7, bf16[52,8,512]{2,1,0:T(8,128)(2,1)} %filters_hbm.1, bf16[256,384]{1,0:T(8,128)(2,1)} %constant.2.clone.steps_hbm), custom_call_target="tpu_custom_call" | custom-call | tf_op jit(solution)/shard_map/detect/pallas_call | solution.py:495
  28.8 0.8 %add.3 = f32[52,2048]{1,0:T(8,128)} add(f32[52,2048]{1,0:T(8,128)S(1)} %get-tuple-element.7, f32[52,2048]{1,0:T(8,128)S(1)} %get-tuple-element.8) | non-fusion elementwise | flops 106496 | bytes 1277952 | tf_op jit(solution)/shard_map/add | solution.py:545
